TPU v7x, 128 devices: a whole 4x4x4 slice. The times are simulated.
128 devices in a mesh: dp: 16 (over z, y), narrow: 8 (over x, core).
Axes of the slice: x: 4, y: 4, z: 4, core: 2. Of those that a mesh axis runs over, the one named last changes fastest.
Arguments:
- waveforms: float32 [256, 16000], P(('dp', 'narrow'))
- valid_counts: int32 [256], P(('dp', 'narrow')), may hold values from 0 to 16000, as said below
- balance_list: int32 [256], P(('dp', 'narrow')), may hold values from -1 to 7, as said below
- cotangent: bfloat16 [128, 49, 512], P(('dp', 'narrow')), may hold values from -0.52734375 to 0.52734375
- w_first: bfloat16 [10, 512], replicated, may hold values from -2 to 2
- w_three: bfloat16 [4, 3, 512, 512], replicated, may hold values from -0.15625 to 0.15625
- w_two: bfloat16 [2, 2, 512, 512], replicated, may hold values from -0.1875 to 0.1875
- conv_bias: float32 [7, 512], replicated, may hold values from -3 to 3
- norm_gain: float32 [7, 512], replicated, may hold values from 0.1 to 1.9
- norm_shift: float32 [7, 512], replicated, may hold values from -3 to 3
Outputs:
- grad_flat: float32 [4210176], P(('dp', 'narrow'))
Inputs may be any that keep to these rules, and one draw needn't show every extreme that they name: `balance_list`: within each group of 8 devices sharing a dp index, exactly half of the group's slots are filled, and each of the group's 8 * 1 compute slots is named by exactly one filled slot; empty slots hold -1. `valid_counts`: 0 exactly on empty slots; filled slots hold at least 4000, and one filled slot of every group holds 16000.
All inputs are finite; a program needn't handle non-finite values.
Results may differ from a plain program's by a relative error of at most 0.02.
Values may be sent and summed in bfloat16 or wider, within the bound.
A program may use at most 192 MiB of HBM per device.

v0:
```python
import jax
import jax.numpy as jnp
from jax import lax
from jax.sharding import PartitionSpec as P

layer_plan = ((10, 5), (3, 2), (3, 2), (3, 2), (3, 2), (2, 2), (2, 2))


def layer_weight(w_first, w_three, w_two, layer):
    if layer == 0:
        return w_first[:, None, :]
    if layer < 5:
        return w_three[layer - 1]
    return w_two[layer - 5]


def post_conv(conv_out, bias_row, gain_row, shift_row):
    shifted = conv_out + bias_row
    average = jnp.mean(shifted, axis=-1, keepdims=True)
    centred = shifted - average
    spread = jnp.mean(centred * centred, axis=-1, keepdims=True)
    normed = centred * lax.rsqrt(spread + 1e-05) * gain_row + shift_row
    return jax.nn.gelu(normed, approximate=False)


def split_weight(weight, stride):
    kernel, in_width, width = weight.shape
    w_head = weight[:stride].reshape(stride * in_width, width)
    w_tail = None
    if kernel > stride:
        w_tail = jnp.pad(weight[stride:], ((0, 2 * stride - kernel), (0, 0), (0, 0))).reshape(
            stride * in_width, width
        )
    return (w_head, w_tail)


def forward_layer(inputs, weight, stride):
    batch_size, length, in_width = inputs.shape
    kernel = weight.shape[0]
    frames = (length - kernel) // stride + 1
    row_count = (frames + 1) * stride
    trimmed = inputs
    trimmed = jnp.pad(trimmed, ((0, 0), (0, row_count - trimmed.shape[1]), (0, 0)))
    packed = trimmed.reshape(batch_size, frames + 1, stride * in_width)
    w_head, w_tail = split_weight(weight, stride)
    conv_out = jnp.einsum(
        "btk,kc->btc", packed[:, :frames], w_head, preferred_element_type=jnp.float32
    )
    if w_tail is not None:
        conv_out = conv_out + jnp.einsum(
            "btk,kc->btc", packed[:, 1:], w_tail, preferred_element_type=jnp.float32
        )
    return (conv_out, packed)


def backward_layer(
    grad_out, conv_out, packed, weight, stride, bias_row, gain_row, shift_row, length, need_input
):
    kernel, in_width, width = weight.shape
    frames = conv_out.shape[1]
    batch_size = conv_out.shape[0]
    unused, pullback = jax.vjp(post_conv, conv_out, bias_row, gain_row, shift_row)
    grad_conv, grad_bias, grad_gain, grad_shift = pullback(grad_out.astype(jnp.float32))
    grad_low = grad_conv.astype(jnp.bfloat16)
    pieces = [
        jnp.einsum(
            "btk,btc->kc", packed[:, :frames], grad_low, preferred_element_type=jnp.float32
        ).reshape(stride, in_width, width)
    ]
    if kernel > stride:
        tail_grad = jnp.einsum(
            "btk,btc->kc", packed[:, 1:], grad_low, preferred_element_type=jnp.float32
        )
        pieces.append(tail_grad.reshape(stride, in_width, width)[: kernel - stride])
    grad_weight = jnp.concatenate(pieces, axis=0)
    grad_input = None
    if need_input:
        w_head, w_tail = split_weight(weight, stride)
        head_part = jnp.einsum("btc,kc->btk", grad_low, w_head, preferred_element_type=jnp.float32)
        scattered = jnp.pad(head_part, ((0, 0), (0, 1), (0, 0)))
        if w_tail is not None:
            tail_part = jnp.einsum(
                "btc,kc->btk", grad_low, w_tail, preferred_element_type=jnp.float32
            )
            scattered = scattered + jnp.pad(tail_part, ((0, 0), (1, 0), (0, 0)))
        grad_input = scattered.reshape(batch_size, (frames + 1) * stride, in_width)[
            :, :length
        ].astype(jnp.bfloat16)
    return (grad_weight, grad_bias, grad_gain, grad_shift, grad_input)


def normalize_wave(waveforms, lengths):
    positions = jnp.arange(waveforms.shape[1], dtype=jnp.int32)
    valid = (positions[None, :] < lengths[:, None]).astype(jnp.float32)
    divisor = jnp.maximum(lengths, 1).astype(jnp.float32)
    average = jnp.sum(waveforms * valid, axis=1) / divisor
    centred = (waveforms - average[:, None]) * valid
    spread = jnp.sum(centred * centred, axis=1) / divisor
    return (centred * lax.rsqrt(spread + 1e-07)[:, None]).astype(jnp.bfloat16)[:, :, None]


def encoder_grads(
    waveforms,
    lengths,
    grad_feat,
    w_first,
    w_three,
    w_two,
    conv_bias,
    norm_gain,
    norm_shift,
    padding,
):
    inputs = normalize_wave(waveforms, lengths)
    saved = []
    frame_len = lengths
    for layer in range(7):
        kernel, stride = layer_plan[layer]
        weight = layer_weight(w_first, w_three, w_two, layer)
        conv_out, packed = forward_layer(inputs, weight, stride)
        saved.append((conv_out, packed, inputs.shape[1]))
        inputs = post_conv(conv_out, conv_bias[layer], norm_gain[layer], norm_shift[layer]).astype(
            jnp.bfloat16
        )
        frame_len = (frame_len - kernel) // stride + 1
    positions = jnp.arange(grad_feat.shape[1], dtype=jnp.int32)
    frame_mask = (positions[None, :] < frame_len[:, None]).astype(jnp.bfloat16)
    grad_out = grad_feat * frame_mask[:, :, None]
    weight_grads = [None] * 7
    bias_grads = [None] * 7
    gain_grads = [None] * 7
    shift_grads = [None] * 7
    for layer in range(6, -1, -1):
        kernel, stride = layer_plan[layer]
        weight = layer_weight(w_first, w_three, w_two, layer)
        conv_out, packed, length = saved[layer]
        outcome = backward_layer(
            grad_out,
            conv_out,
            packed,
            weight,
            stride,
            conv_bias[layer],
            norm_gain[layer],
            norm_shift[layer],
            length,
            layer > 0,
        )
        weight_grads[layer], bias_grads[layer], gain_grads[layer], shift_grads[layer], grad_out = (
            outcome
        )
    pieces = [weight_grads[0].reshape(-1)]
    pieces += [weight_grads[layer].reshape(-1) for layer in range(1, 7)]
    pieces += [
        jnp.stack(bias_grads).reshape(-1),
        jnp.stack(gain_grads).reshape(-1),
        jnp.stack(shift_grads).reshape(-1),
    ]
    pieces.append(jnp.zeros((padding,), jnp.float32))
    return jnp.concatenate(pieces)


def on_device(
    waveforms,
    valid_counts,
    balance_list,
    cotangent,
    w_first,
    w_three,
    w_two,
    conv_bias,
    norm_gain,
    norm_shift,
):
    device_count = lax.axis_size("dp") * lax.axis_size("narrow")
    width = w_three.shape[-1]
    param_count = 16 * width * width + 31 * width
    padding = (device_count - param_count % device_count) % device_count
    compute_slots = cotangent.shape[0]
    my_slots = lax.axis_index("narrow") * compute_slots + jnp.arange(compute_slots, dtype=jnp.int32)
    wave_piece = lax.all_gather(waveforms, "narrow", axis=0, tiled=True)
    count_piece = lax.all_gather(valid_counts, "narrow", axis=0, tiled=True)
    dest_piece = lax.all_gather(balance_list, "narrow", axis=0, tiled=True)
    matches = dest_piece[None, :] == my_slots[:, None]
    chosen_waves = jnp.sum(jnp.where(matches[:, :, None], wave_piece[None, :, :], 0.0), axis=1)
    picked_counts = jnp.sum(jnp.where(matches, count_piece[None, :], 0), axis=1).astype(jnp.int32)

    def one_block(total, items):
        wave_row, count_one, feat_one = items
        term = encoder_grads(
            wave_row[None],
            count_one[None],
            feat_one[None],
            w_first,
            w_three,
            w_two,
            conv_bias,
            norm_gain,
            norm_shift,
            padding,
        )
        return (total + term, None)

    zero_total = jnp.zeros((param_count + padding,), jnp.float32)
    flat_grads, unused = lax.scan(one_block, zero_total, (chosen_waves, picked_counts, cotangent))
    result = lax.psum_scatter(flat_grads, ("dp", "narrow"), scatter_dimension=0, tiled=True)
    return result


def solution(mesh):
    in_specs = (
        P(("dp", "narrow"), None),
        P(("dp", "narrow")),
        P(("dp", "narrow")),
        P(("dp", "narrow"), None, None),
        P(),
        P(),
        P(),
        P(),
        P(),
        P(),
    )
    out_specs = P(("dp", "narrow"))
    return jax.shard_map(
        on_device, mesh=mesh, in_specs=in_specs, out_specs=out_specs, check_vma=False
    )
```

profile of v0, /device:TPU:0, one launch (start us, length us, event | category | flops | bytes accessed | tf_op | source)
XLA Modules:
  0.0 522.8 jit_solution(9103866041394069819)
XLA Ops:
  10.1 9.3 %all-reduce.23 = (s32[16]{0:T(128)S(1)}, s32[16]{0:T(128)S(1)}) all-reduce(s32[16]{0:T(128)S(1)} %dynamic-update-slice, s32[16]{0:T(128)S(1)} %dynamic-update-slice.1), channel_id=1, replica_groups=mesh['dp'=16,'narrow'=8] {'narrow'}, use_global_device_ids=true, to_apply=%add.20 | all-reduce | flops 32 | bytes 256
  21.3 2.9 slice_bitcast_fusion.12
  24.2 4.4 fusion.210
  29.1 13.9 %all-gather = f32[8,2,16000]{2,1,0:T(2,128)S(1)} all-gather(f32[1,2,16000]{2,1,0:T(2,128)S(1)} %bitcast.458), channel_id=1, replica_groups=mesh['dp'=16,'narrow'=8] {'narrow'}, dimensions={0}, use_global_device_ids=true | all-gather | bytes 1152000 | tf_op jit(solution)/shard_map/all_gather | solution.py:181
  55.9 17.1 %fusion.23 = (bf16[1,3199,512]{1,2,0:T(8,128)(2,1)}, f32[3199,512]{0,1:T(8,128)}) fusion(f32[3199,512]{0,1:T(8,128)S(1)} %get-tuple-element.146, f32[512]{0:T(512)S(1)} %bitcast.479, f32[512]{0:T(512)S(1)} %bitcast.459, f32[3199]{0:T(1024)S(1)} %fusion.175, f32[3199]{0:T(1024)S(1)} %broadcast_multiply_fusion), kind=kLoop, calls=%fused_computation.50 | loop fusion | flops 113014272 | bytes 16408568 | tf_op jit(solution)/shard_map/while/body/eval_jaxpr/convert_element_type | solution.py:122
  73.0 4.0 copy.27
  78.9 4.7 reshape.1534
  87.1 4.1 fusion.216
  91.8 9.7 %fusion.43 = (bf16[1,1599,512]{2,1,0:T(8,128)(2,1)S(1)}, f32[1599,512]{1,0:T(8,128)}) fusion(f32[1599,512]{1,0:T(8,128)S(1)} %get-tuple-element.148, f32[512]{0:T(512)S(1)} %bitcast.481, f32[512]{0:T(512)S(1)} %bitcast.474, f32[1599]{0:T(1024)S(1)} %fusion.178, f32[1599]{0:T(1024)S(1)} %broadcast_multiply_fusion.1), kind=kLoop, calls=%fused_computation.97 | loop fusion | flops 56489472 | bytes 8203768 | tf_op jit(solution)/shard_map/while/body/eval_jaxpr/convert_element_type | solution.py:122
  102.8 3.6 reshape.1539
  107.6 2.9 fusion.188
  112.8 5.2 %fusion.91 = (bf16[1,799,512]{2,1,0:T(8,128)(2,1)S(1)}, f32[799,512]{1,0:T(8,128)}) fusion(f32[799,512]{1,0:T(8,128)S(1)} %get-tuple-element.150, f32[512]{0:T(512)S(1)} %bitcast.483, f32[512]{0:T(512)S(1)} %bitcast.462, f32[799]{0:T(1024)S(1)} %fusion.179, f32[799]{0:T(1024)S(1)} %broadcast_multiply_fusion.2), kind=kLoop, calls=%fused_computation.174 | loop fusion | flops 28227072 | bytes 4101368 | tf_op jit(solution)/shard_map/while/body/eval_jaxpr/convert_element_type | solution.py:122
  122.5 2.4 fusion.99
  126.6 2.9 fusion.117
  139.4 2.8 fusion.211
  164.8 2.4 fusion.119
  173.7 3.1 fusion.93
  184.6 4.4 fusion.46
  195.1 3.7 reshape.1567
  198.8 5.9 %fusion.24 = (f32[512]{0:T(512)}, f32[1599]{0:T(1024)S(1)}, f32[512]{0:T(512)}, f32[1,1599,512]{2,1,0:T(8,128)S(1)}) fusion(f32[1599,512]{1,0:T(8,128)S(1)} %get-tuple-element.148, f32[1599]{0:T(1024)S(1)} %fusion.178, f32[1599]{0:T(1024)S(1)} %broadcast_multiply_fusion.1, f32[512]{0:T(512)} %bitcast.475, f32[1599,512]{1,0:T(8,128)} %get-tuple-element.91, ...), kind=kLoop, calls=%fused_computation.53 | loop fusion | flops 19645888 | bytes 11494132 | tf_op jit(solution)/shard_map/while/body/eval_jaxpr/transpose(jvp())/reduce_sum | solution.py:22
  214.5 2.4 slice_bitcast_fusion.3
  217.1 4.1 slice_bitcast_fusion.1
  223.0 3.2 reshape.1569
  226.2 4.3 copy.26
  230.6 10.0 %fusion.8 = (f32[512]{0:T(512)}, f32[3199]{0:T(1024)S(1)}, f32[512]{0:T(512)S(1)}, f32[1,3199,512]{1,2,0:T(8,128)S(1)}) fusion(f32[3199,512]{0,1:T(8,128)} %copy-done, f32[3199]{0:T(1024)S(1)} %fusion.175, f32[3199]{0:T(1024)S(1)} %broadcast_multiply_fusion, f32[512]{0:T(512)S(1)} %bitcast.460, f32[3199,512]{0,1:T(8,128)} %get-tuple-element.93, ...), kind=kLoop, calls=%fused_computation.14 | loop fusion | flops 39305088 | bytes 22977012 | tf_op jit(solution)/shard_map/while/body/eval_jaxpr/transpose(jvp())/reduce_sum | solution.py:22
  251.7 2.5 copy.31
  256.3 2.5 copy.30
  259.7 2.6 fusion.55
  263.4 2.4 copy.29
  265.9 3.9 copy.20
  269.8 4.7 fusion.47
  296.1 217.9 %all-reduce.26.cloned.1.call-done = f32[4210176]{0:T(1024)} async-done(((f32[4210176]{0:T(1024)}), f32[4210176]{0:T(1024)}) %all-reduce.26.cloned.1.call-update) | async-done | bytes 16840720
  (400 shorter events, 134.4 us)
Async XLA Ops:
  6.5 507.5 %all-reduce.26.cloned.1.call-start = ((), (), s32[]{:S(2)}) async-start(), calls=%async_computation | async-start | bytes 33685504
  24.2 5.0 copy-start.58
  28.6 20.7 %copy-start.90 = (f32[7,512]{1,0:T(8,128)S(1)}, f32[7,512]{1,0:T(8,128)}, u32[]{:S(2)}) copy-start(f32[7,512]{1,0:T(8,128)} %param.17) | copy-start | bytes 43012
  43.0 7.8 %copy-start.89 = (bf16[10,512]{1,0:T(8,128)(2,1)S(1)}, bf16[10,512]{1,0:T(8,128)(2,1)}, u32[]{:S(2)}) copy-start(bf16[10,512]{1,0:T(8,128)(2,1)} %param.14) | copy-start | bytes 30724
  55.0 18.0 %copy-start.66 = (f32[1,512]{1,0:T(1,128)}, f32[1,512]{1,0:T(1,128)S(1)}, u32[]{:S(2)}) copy-start(f32[1,512]{1,0:T(1,128)S(1)} %get-tuple-element.136) | copy-start | bytes 6148
  55.0 36.8 %copy-start.75 = (f32[1,512]{1,0:T(1,128)}, f32[1,512]{1,0:T(1,128)S(1)}, u32[]{:S(2)}) copy-start(f32[1,512]{1,0:T(1,128)S(1)} %get-tuple-element.135) | copy-start | bytes 6148
  55.0 57.1 %copy-start.68 = (f32[1,512]{1,0:T(1,128)}, f32[1,512]{1,0:T(1,128)S(1)}, u32[]{:S(2)}) copy-start(f32[1,512]{1,0:T(1,128)S(1)} %get-tuple-element.134) | copy-start | bytes 6148
  55.0 71.0 %copy-start.71 = (f32[1,512]{1,0:T(1,128)}, f32[1,512]{1,0:T(1,128)S(1)}, u32[]{:S(2)}) copy-start(f32[1,512]{1,0:T(1,128)S(1)} %get-tuple-element.133) | copy-start | bytes 6148
  55.0 81.2 %copy-start.70 = (f32[1,512]{1,0:T(1,128)}, f32[1,512]{1,0:T(1,128)S(1)}, u32[]{:S(2)}) copy-start(f32[1,512]{1,0:T(1,128)S(1)} %get-tuple-element.132) | copy-start | bytes 6148
  55.8 17.2 %copy-start.81 = (f32[1,512]{1,0:T(1,128)}, f32[1,512]{1,0:T(1,128)S(1)}, u32[]{:S(2)}) copy-start(f32[1,512]{1,0:T(1,128)S(1)} %get-tuple-element.129) | copy-start | bytes 6148
  55.8 36.0 %copy-start.83 = (f32[1,512]{1,0:T(1,128)}, f32[1,512]{1,0:T(1,128)S(1)}, u32[]{:S(2)}) copy-start(f32[1,512]{1,0:T(1,128)S(1)} %get-tuple-element.128) | copy-start | bytes 6148
  55.8 56.3 %copy-start.84 = (f32[1,512]{1,0:T(1,128)}, f32[1,512]{1,0:T(1,128)S(1)}, u32[]{:S(2)}) copy-start(f32[1,512]{1,0:T(1,128)S(1)} %get-tuple-element.127) | copy-start | bytes 6148
  55.8 70.2 %copy-start.87 = (f32[1,512]{1,0:T(1,128)}, f32[1,512]{1,0:T(1,128)S(1)}, u32[]{:S(2)}) copy-start(f32[1,512]{1,0:T(1,128)S(1)} %get-tuple-element.126) | copy-start | bytes 6148
  55.8 80.5 %copy-start.85 = (f32[1,512]{1,0:T(1,128)}, f32[1,512]{1,0:T(1,128)S(1)}, u32[]{:S(2)}) copy-start(f32[1,512]{1,0:T(1,128)S(1)} %get-tuple-element.125) | copy-start | bytes 6148
  91.8 9.7 %copy-start.61 = (f32[1599]{0:T(1024)}, f32[1599]{0:T(1024)S(1)}, u32[]{:S(2)}) copy-start(f32[1599]{0:T(1024)S(1)} %multiply_reduce_fusion.1) | copy-start | bytes 19192
  111.6 7.4 %copy-start.59 = (f32[799]{0:T(1024)}, f32[799]{0:T(1024)S(1)}, u32[]{:S(2)}) copy-start(f32[799]{0:T(1024)S(1)} %broadcast_multiply_fusion.2) | copy-start | bytes 9592
  112.0 9.3 %copy-start.77 = (f32[799]{0:T(1024)}, f32[799]{0:T(1024)S(1)}, u32[]{:S(2)}) copy-start(f32[799]{0:T(1024)S(1)} %multiply_reduce_fusion.2) | copy-start | bytes 9592
  112.0 9.3 %copy-start.63 = (f32[799]{0:T(1024)}, f32[799]{0:T(1024)S(1)}, u32[]{:S(2)}) copy-start(f32[799]{0:T(1024)S(1)} %fusion.179) | copy-start | bytes 9592
  125.7 9.8 %copy-start.73 = (f32[399]{0:T(512)}, f32[399]{0:T(512)S(1)}, u32[]{:S(2)}) copy-start(f32[399]{0:T(512)S(1)} %broadcast_multiply_fusion.3) | copy-start | bytes 4792
  126.0 9.5 %copy-start.86 = (f32[399]{0:T(512)}, f32[399]{0:T(512)S(1)}, u32[]{:S(2)}) copy-start(f32[399]{0:T(512)S(1)} %multiply_reduce_fusion.3) | copy-start | bytes 4792
  126.0 9.5 %copy-start.79 = (f32[399]{0:T(512)}, f32[399]{0:T(512)S(1)}, u32[]{:S(2)}) copy-start(f32[399]{0:T(512)S(1)} %fusion.180) | copy-start | bytes 4792
  133.3 5.2 %copy-start.20 = (bf16[2,512,512]{2,1,0:T(8,128)(2,1)}, bf16[2,512,512]{2,1,0:T(8,128)(2,1)S(1)}, u32[]{:S(2)}) copy-start(bf16[2,512,512]{2,1,0:T(8,128)(2,1)S(1)} %pad.110) | copy-start | bytes 3145732
  164.8 5.1 copy-start.23
  164.8 5.6 %copy-start.21 = (bf16[2,512,512]{2,1,0:T(8,128)(2,1)S(1)}, bf16[2,512,512]{2,1,0:T(8,128)(2,1)}, u32[]{:S(2)}) copy-start(bf16[2,512,512]{2,1,0:T(8,128)(2,1)} %copy-done.20) | copy-start | bytes 3145732
  173.7 5.6 %copy-start.30 = (bf16[1,2,512,512]{3,2,1,0:T(8,128)(2,1)S(1)}, bf16[1,2,512,512]{3,2,1,0:T(8,128)(2,1)}, u32[]{:S(2)}) copy-start(bf16[1,2,512,512]{3,2,1,0:T(8,128)(2,1)} %get-tuple-element.99) | copy-start | bytes 3145732
  198.8 5.9 %copy-start.62 = (f32[1599]{0:T(1024)S(1)}, f32[1599]{0:T(1024)}, u32[]{:S(2)}) copy-start(f32[1599]{0:T(1024)} %copy-done.61) | copy-start | bytes 19192
  198.8 5.9 %copy-start.76 = (f32[1,512]{1,0:T(1,128)S(1)}, f32[1,512]{1,0:T(1,128)}, u32[]{:S(2)}) copy-start(f32[1,512]{1,0:T(1,128)} %copy-done.75) | copy-start | bytes 6148
  230.5 10.0 %slice-start = ((s8[6553600]{0:T(1024)(128)(4,1)}), s8[4194304]{0:T(1024)(128)(4,1)S(1)}, s32[]{:S(2)}) async-start(s8[6553600]{0:T(1024)(128)(4,1)} %bitcast.424), calls=%async_computation.1 | async-start | bytes 8388608
  230.6 10.0 %slice-start.1 = ((s8[6553600]{0:T(1024)(128)(4,1)}), s8[2359296]{0:T(1024)(128)(4,1)S(1)}, s32[]{:S(2)}) async-start(s8[6553600]{0:T(1024)(128)(4,1)} %bitcast.424), calls=%async_computation.2 | async-start | bytes 4718592
  245.7 4.6 copy-start.45
  269.7 4.7 copy-start.34
  269.8 4.7 copy-start.43
  (91 other events, 244.5 us)
Sparse Core Ops, SparseCore 0:
  296.2 217.7 all-reduce.25
where the time goes:
time: 531 us; the launch traced here: 523 us
  waiting for transfers between devices  218 us (41%)
  local copies, waits for them, and re-layouts  117 us (22%)
  other arithmetic  97.1 us (18%)
  matrix products  48.8 us (9%)
  blocking collectives  23.2 us (4%)
  between operations  18.6 us (4%)
    unnamed x2, waiting for transfers between devices  218 us
    unnamed x268, local copies, waits for them, and re-layouts  48.1 us
    convert_element_type x6, other arithmetic, encoder_grads(): post_conv(conv_out, conv_bias[layer], norm_gain[layer], norm_shift[layer])  38.6 us
    reduce_sum x7, other arithmetic, post_conv(): normed = centred * lax.rsqrt(spread + 1e-05) * gain_row + shift_row  29.4 us
    reshape x6, local copies, waits for them, and re-layouts, forward_layer(): packed = trimmed.reshape(batch_size, frames + 1, stride * in_width)  14.8 us
    dot_general x8, local copies, waits for them, and re-layouts, backward_layer(): jnp.einsum('btk,btc->kc', packed[:, :frames], grad_low, preferred_element...  14.5 us
    all_gather x1, blocking collectives, on_device(): wave_piece = lax.all_gather(waveforms, 'narrow', axis=0, tiled=True)  13.9 us
    dot_general x7, matrix products, forward_layer(): jnp.einsum('btk,kc->btc', packed[:, :frames], w_head, preferred_element_t...  13.5 us
  transfers between devices with their start and end apart: 1, of which 1 were waited for; matrix products, arithmetic and copies ran while one was open for 0% of the time, Pallas kernels for 0%

commit v1 on v0

v1 whole, which is shorter than its diff:
```python
import jax
import jax.numpy as jnp
from jax import lax
from jax.experimental import pallas as pl
from jax.experimental.pallas import tpu as pltpu
from jax.sharding import PartitionSpec as P

C = 512
F7 = 49
BF = jnp.bfloat16
F32 = jnp.float32

taps = (None, 3, 3, 3, 3, 2, 2)
phases = (8, 4, 2, 1, 1, 1, 1)
rows_of = (400, 400, 400, 400, 208, 112, 64)
in_blocks = (None, 9, 5, 3, 3, 2, 2)
ROW_TILE = {400: 400, 208: 208, 112: 112, 64: 64}


def dot(a, b):
    return jnp.dot(a, b, preferred_element_type=F32)


def dot_bt(a, b):
    return lax.dot_general(a, b, (((1,), (1,)), ((), ())), preferred_element_type=F32)


def dot_at(a, b):
    return lax.dot_general(a, b, (((0,), (0,)), ((), ())), preferred_element_type=F32)


def gelu_pair(n):
    e = jnp.exp(n * n * -0.5)
    t = 1.0 / (1.0 + jnp.abs(n) * (0.3275911 * 0.7071067811865476))
    poly = 0.5 * 1.061405429
    for a in (-1.453152027, 1.421413741, -0.284496736, 0.254829592):
        poly = poly * t + 0.5 * a
    half = poly * t * e
    phi = jnp.where(n >= 0, 1.0 - half, half)
    x = n * phi
    return x, phi + (n * 0.3989422804014327) * e


def loop_rows(rows, body, init):
    tile = ROW_TILE[rows]

    def step(i, carry):
        return body(pl.ds(pl.multiple_of(i * tile, tile), tile), carry)

    return lax.fori_loop(0, rows // tile, step, init)


def fold8(v):
    total = v[0:8]
    for i in range(8, v.shape[0], 8):
        total = total + v[i : i + 8]
    return total


def encoder_body(
    route, cot, w1, w3_hbm, w2_hbm, bias, gain, shift,
    emit, between, small,
    a0, w3, w2, wb, gw, x_refs, dg_refs, xh_refs, rs_refs, zs, zt, fs, f4, dz, gn, acc, bb, mm, bandf, wsem,
):
    w_copies = []
    for i in range(4):
        w_copies.append(pltpu.make_async_copy(w3_hbm.at[i], w3.at[i], wsem.at[i]))
    for i in range(2):
        w_copies.append(pltpu.make_async_copy(w2_hbm.at[i], w2.at[i], wsem.at[4 + i]))
    for c in w_copies:
        c.start()

    def weight(l, k):
        if l < 5:
            return w3[l - 1, k * C : (k + 1) * C, :]
        return w2[l - 5, k * C : (k + 1) * C, :]

    wf = w1[...].astype(F32)
    wc = wf - jnp.mean(wf, axis=-1, keepdims=True)
    b0 = bias[0:1, :]
    bc = b0 - jnp.mean(b0, axis=-1, keepdims=True)
    g0 = gain[0:1, :]

    def split(v):
        hi = v.astype(BF).astype(F32)
        return hi, v - hi

    wc_hi, wc_lo = split(wc)
    bc_hi, bc_r = split(bc)
    bc_mid, bc_lo = split(bc_r)
    gw_hi, gw_lo = split(wc * g0)
    gb_hi, gb_lo = split(bc * g0)
    g_hi, g_lo = split(g0)
    for p in range(8):
        bandf[...] = jnp.zeros_like(bandf)
        bandf[5 * p : 5 * p + 10, :] = wc_hi
        bandf[45 + 5 * p : 55 + 5 * p, :] = wc_lo
        bandf[90:91, :] = bc_hi
        bandf[91:92, :] = bc_mid
        bandf[92:93, :] = bc_lo
        wb[:, p * C : (p + 1) * C] = bandf[...].astype(BF)
        bandf[5 * p : 5 * p + 10, :] = gw_hi
        bandf[45 + 5 * p : 55 + 5 * p, :] = gw_lo
        bandf[90:91, :] = gb_hi
        bandf[91:92, :] = gb_lo
        bandf[92:93, :] = jnp.zeros_like(bc_lo)
        bandf[126:127, :] = g_hi
        bandf[127:128, :] = g_lo
        gw[:, p * C : (p + 1) * C] = bandf[...].astype(BF)

    fs[400:424, :] = jnp.zeros((24, C), F32)
    f4[:, 400:424, :] = jnp.zeros((4, 24, 128), F32)

    last_frames = route()

    def activate(l, p, centred):
        rows = rows_of[l]
        lanes = pl.ds(pl.multiple_of(p * C, C), C)
        b = bias[l : l + 1, :]
        g = gain[l : l + 1, :]
        s = shift[l : l + 1, :]

        def body(r, carry):
            z = zs[r, :]
            if not centred:
                z = z + b
                z = z - jnp.sum(z, axis=-1, keepdims=True) * (1.0 / C)
            var = jnp.sum(z * z, axis=-1, keepdims=True) * (1.0 / C)
            rstd = lax.rsqrt(var + 1e-05)
            xh = z * rstd
            x, d = gelu_pair(xh * g + s)
            dg_refs[l][r, lanes] = d.astype(BF)
            if l > 0:
                xh_refs[l][r, lanes] = xh.astype(BF)
            rs_refs[l][p, r, :] = jnp.broadcast_to(rstd, (rstd.shape[0], 128))
            if l < 3:
                x_refs[l + 1][r, lanes] = x.astype(BF)
            if l < 3:
                fs[r, :] = x
            elif l < 6:
                for c in range(4):
                    f4[c, r, :] = x[:, c * 128 : (c + 1) * 128]
            return carry

        loop_rows(rows, body, 0)
        if l < 3:
            @pl.when(p == 0)
            def _():
                n = phases[l]
                x_refs[l + 1][:, n * C : (n + 1) * C] = fs[pl.ds(1, 400), :].astype(BF)

    def first(p, carry):
        lanes = pl.ds(pl.multiple_of(p * C, C), C)
        zs[...] = dot(a0[...], wb[:, lanes])
        activate(0, p, True)
        return carry

    lax.fori_loop(0, 8, first, 0)

    for l in range(1, 7):
        w_copies[l - 1].wait()
        k, rows = taps[l], rows_of[l]

        def conv(p, carry, l=l, k=k, rows=rows):
            x = x_refs[l][:, pl.ds(pl.multiple_of(p * 2 * C, 2 * C), k * C)]
            w = w3[l - 1] if l < 5 else w2[l - 5]
            zs[0:rows, :] = dot(x, w)
            activate(l, p, False)
            return carry

        if phases[l] > 1:
            lax.fori_loop(0, phases[l], conv, 0)
        else:
            conv(0, 0)
        if 3 <= l < 6:
            n = rows_of[l + 1]
            for j in range(taps[l + 1]):
                for c in range(4):
                    x_refs[l + 1][:, j * C + c * 128 : j * C + (c + 1) * 128] = f4[
                        c, pl.ds(j, n, stride=2), :
                    ].astype(BF)

    row_id = lax.broadcasted_iota(jnp.int32, (F7, C), 0).astype(F32)
    zs[0:64, :] = jnp.zeros((64, C), F32)
    zs[0:F7, :] = jnp.where(row_id < last_frames, cot[0].astype(F32), 0.0)

    def got(src, r):
        if src is None:
            return jnp.concatenate([f4[c, r, :] for c in range(4)], axis=-1)
        return src[r, :]

    def norm_back(l, p, src, sums):
        lanes = pl.ds(pl.multiple_of(p * C, C), C)
        out = pl.ds(pl.multiple_of((p + 1) * C, C), C)
        g = gain[l : l + 1, :]

        def body(r, carry):
            db, dga, dsh = carry
            gv = got(src, r) * dg_refs[l][r, lanes].astype(F32)
            xh = xh_refs[l][r, lanes].astype(F32)
            rstd = rs_refs[l][p, r, :][:, 0:1]
            dsh = dsh + fold8(gv)
            dga = dga + fold8(gv * xh)
            gx = gv * g
            m1 = jnp.sum(gx, axis=-1, keepdims=True) * (1.0 / C)
            m2 = jnp.sum(gx * xh, axis=-1, keepdims=True) * (1.0 / C)
            d = (gx - m1 - xh * m2) * rstd
            db = db + fold8(d)
            dz[r, out] = d.astype(BF)
            return db, dga, dsh

        return loop_rows(rows_of[l], body, sums)

    zero8 = jnp.zeros((8, C), F32)
    sums = norm_back(6, 0, zs, (zero8, zero8, zero8))

    def store_sums(l, sums):
        for j in range(3):
            small[10 + 7 * j + l : 11 + 7 * j + l, :] = jnp.sum(sums[j], axis=0, keepdims=True)

    for l in range(6, 0, -1):
        k, rows, n = taps[l], rows_of[l], phases[l]
        store_sums(l, sums)
        if k == 3:
            fs[8 : 8 + rows, :] = dz[0:rows, n * C : (n + 1) * C].astype(F32)
            fs[0:8, :] = jnp.zeros((8, C), F32)
            dz[0:rows, 0:C] = fs[pl.ds(7, rows), :].astype(BF)

        def wgrad(p, carry, l=l, k=k, rows=rows):
            x = x_refs[l][:, pl.ds(pl.multiple_of(p * 2 * C, 2 * C), k * C)]
            d = dz[0:rows, pl.ds(pl.multiple_of((p + 1) * C, C), C)]
            for j in range(k):
                part = dot_at(x[:, j * C : (j + 1) * C], d)
                if isinstance(p, int):
                    acc[j * C : (j + 1) * C, :] = part
                else:
                    acc[j * C : (j + 1) * C, :] += part
            return carry

        wgrad(0, 0)
        if n > 1:
            lax.fori_loop(1, n, wgrad, 0)
        emit(l, acc)

        if l > 3:
            here = dz[0:rows, C : 2 * C]
            even = dot_bt(here, weight(l, 0))
            if k == 3:
                even = even + dot_bt(dz[0:rows, 0:C], weight(l, 2))
            odd = dot_bt(here, weight(l, 1))
            half = rows_of[l - 1] // 2
            for c in range(4):
                f4[c, pl.ds(0, half, stride=2), :] = even[:half, c * 128 : (c + 1) * 128]
                f4[c, pl.ds(1, half, stride=2), :] = odd[:half, c * 128 : (c + 1) * 128]
            sums = norm_back(l - 1, 0, None, (zero8, zero8, zero8))
            between(l)
        elif l > 1:
            def dgrad(p, carry, l=l):
                here = dz[:, pl.ds(pl.multiple_of((p + 1) * C, C), C)]
                before = dz[:, pl.ds(pl.multiple_of(p * C, C), C)]
                zt[2 * p] = dot_bt(here, weight(l, 0)) + dot_bt(before, weight(l, 2))
                zt[2 * p + 1] = dot_bt(here, weight(l, 1))
                return carry

            for p in range(n):
                dgrad(p, 0)

            def back(p, carry, l=l):
                return norm_back(l - 1, p, zt.at[p], carry)

            sums = lax.fori_loop(0, 2 * n, back, (zero8, zero8, zero8))
            between(l)
        else:
            def first_back(p, dsh):
                def one(q, src, dsh):
                    lanes = pl.ds(pl.multiple_of(q * C, C), C)
                    zs[...] = src

                    def body(r, dsh):
                        gv = zs[r, :] * dg_refs[0][r, lanes].astype(F32)
                        dsh = dsh + fold8(gv)
                        gn[r, 0:C] = (gv * rs_refs[0][q, r, :][:, 0:1]).astype(BF)
                        return dsh

                    dsh = loop_rows(400, body, dsh)
                    u = dot_bt(gn[:, 0:C], gw[:, lanes])
                    a = a0[...].astype(F32)
                    lane = lax.broadcasted_iota(jnp.int32, (400, 128), 1)
                    m2 = jnp.sum(a * u, axis=-1, keepdims=True) * (1.0 / C)
                    m1 = jnp.sum(jnp.where(lane >= 126, u, 0.0), axis=-1, keepdims=True) * (1.0 / C)
                    rstd = rs_refs[0][q]
                    rhs = jnp.where(lane == 127, m1, a * (rstd * rstd * m2))
                    hi = rhs.astype(BF)
                    gn[:, C : C + 128] = hi
                    gn[:, C + 128 : C + 256] = (rhs - hi.astype(F32)).astype(BF)
                    both = dot_at(a0[...], gn[...])
                    bb[lax.rem(q, 4), pl.ds(pl.multiple_of(lax.div(q, 4) * 128, 128), 128), :] = both[:, 0:C]
                    mm[q] = both[:, C : C + 128] + both[:, C + 128 : C + 256]
                    return dsh

                here = dz[:, pl.ds(pl.multiple_of((p + 1) * C, C), C)]
                before = dz[:, pl.ds(pl.multiple_of(p * C, C), C)]
                dsh = one(2 * p, dot_bt(here, weight(1, 0)) + dot_bt(before, weight(1, 2)), dsh)
                dsh = one(2 * p + 1, dot_bt(here, weight(1, 1)), dsh)
                for i in range(4):
                    @pl.when(p == i)
                    def _(i=i):
                        between(("first", i))
                return dsh

            dsh = lax.fori_loop(0, 4, first_back, zero8)
            dw = jnp.zeros((10, C), F32)
            db = jnp.zeros((1, C), F32)
            dga = jnp.zeros((1, C), F32)
            for q in range(8):
                bq = bb[q % 4, q // 4 * 128 : q // 4 * 128 + 128, :]
                band = wb[:, q * C : (q + 1) * C].astype(F32)
                dga = dga + jnp.sum(bq * band, axis=0, keepdims=True)
                m = mm[q]
                bandf[...] = bq * g0 - m[:, 127:128] - jnp.dot(
                    m, band, preferred_element_type=F32, precision=lax.Precision.HIGHEST
                )
                dw = dw + bandf[5 * q : 5 * q + 10, :]
                db = db + bandf[90:91, :]
            small[0:10, :] = dw
            small[10:11, :] = db
            small[17:18, :] = dga
            small[24:25, :] = jnp.sum(dsh, axis=0, keepdims=True)
            small[31:32, :] = jnp.zeros((1, C), F32)


def body_scratch():
    s = [
        pltpu.VMEM((400, 128), BF),
        pltpu.VMEM((4, 3 * C, C), BF),
        pltpu.VMEM((2, 2 * C, C), BF),
        pltpu.VMEM((128, 8 * C), BF),
        pltpu.VMEM((128, 8 * C), BF),
    ]
    s.append([pltpu.VMEM((rows_of[l], in_blocks[l] * C), BF) for l in range(1, 7)])
    s.append([pltpu.VMEM((rows_of[l], phases[l] * C), BF) for l in range(7)])
    s.append([pltpu.VMEM((rows_of[l], phases[l] * C), BF) for l in range(1, 7)])
    s.append([pltpu.VMEM((phases[l], rows_of[l], 128), F32) for l in range(7)])
    s += [
        pltpu.VMEM((400, C), F32),
        pltpu.VMEM((4, 400, C), F32),
        pltpu.VMEM((424, C), F32),
        pltpu.VMEM((4, 424, 128), F32),
        pltpu.VMEM((400, 5 * C), BF),
        pltpu.VMEM((400, C + 256), BF),
        pltpu.VMEM((3 * C, C), F32),
        pltpu.VMEM((8, 128, 128), F32),
        pltpu.VMEM((128, C), F32),
        pltpu.SemaphoreType.DMA((6,)),
    ]
    return s


MESH = pl.DeviceIdType.MESH
SHARD = 32892
ORDERS = (("x", "y", "z"), ("y", "z", "x"), ("z", "x", "y"))


def unit_of(l, k):
    return (l - 1) * 3 + k if l < 5 else 12 + (l - 5) * 2 + k


def order_of(l, k):
    return ORDERS[(k + (2 if l == 6 else 0)) % 3]


def first_tile(d):
    return lax.div(SHARD * d + 3072, 8192) - 1


def encoder_kernel(
    packed, bal, cot, w1, w3_hbm, w2_hbm, bias, gain, shift, out, *scratch
):
    (a0, w3, w2, wb, gw, xs, dgs, xhs, rss, zs, zt, fs, f4, dz, gn, acc, mm, bandf, wsem,
     small, sb, rb, xr, s0, keep, r0, r1, h2, r2, h3, r3, tl, own, fl, rs0, hs, rs1, ts, root, root0, sm4,
     sb_sem, rb_sem, s0_sem, r0_sem, s1_sem, r1_sem, s2_sem, r2_sem, s3_sem, r3_sem, t_sem, own_sem,
     q_send, q_recv, root_sem, qr_send) = scratch

    dp = lax.axis_index("dp")
    nw = lax.axis_index("narrow")
    z, y = lax.div(dp, 4), lax.rem(dp, 4)
    x, core = lax.div(nw, 2), lax.rem(nw, 2)
    me = dp * 8 + nw
    at = {"x": x, "y": y, "z": z}

    def peer(axis, delta):
        if axis == "core":
            return (dp, x * 2 + (1 - core))
        if axis == "x":
            return (dp, lax.rem(x + delta, 4) * 2 + core)
        if axis == "y":
            return (z * 4 + lax.rem(y + delta, 4), nw)
        return (lax.rem(z + delta, 4) * 4 + y, nw)

    def remote(src, dst, send, recv, device):
        return pltpu.make_async_remote_copy(
            src_ref=src, dst_ref=dst, send_sem=send, recv_sem=recv, device_id=device, device_id_type=MESH
        )

    barrier = pltpu.get_barrier_semaphore()
    for d in range(1, 8):
        pl.semaphore_signal(barrier, inc=1, device_id=(dp, lax.rem(nw + d, 8)), device_id_type=MESH)
    for axis in ("y", "z"):
        for d in range(1, 4):
            pl.semaphore_signal(barrier, inc=1, device_id=peer(axis, d), device_id_type=MESH)

    def route():
        for d in range(8):
            there = lax.rem(nw + d, 8)
            m0 = jnp.where(bal[0] == there, 1.0, 0.0)
            m1 = jnp.where(bal[1] == there, 1.0, 0.0)
            sb[d] = (packed[0].astype(F32) * m0 + packed[1].astype(F32) * m1).astype(BF)
        pl.semaphore_wait(barrier, 13)
        copies = []
        for d in range(1, 8):
            c = remote(sb.at[d], rb.at[d - 1], sb_sem.at[d - 1], rb_sem.at[d - 1], (dp, lax.rem(nw + d, 8)))
            c.start()
            copies.append(c)
        g = sb[0].astype(F32)
        for d in range(1, 8):
            copies[d - 1].wait()
            g = g + rb[d - 1].astype(F32)
        for b in range(3):
            xr[144 * b : 144 * b + 144, :] = g if b == 0 else pltpu.roll(g, 128 - 40 * b, 1)
        xr[432:440, :] = jnp.zeros((8, 128), F32)
        v0 = xr[0:400, :]
        v1 = pltpu.roll(xr[pl.ds(1, 400), :], 40, 1)
        lane = lax.broadcasted_iota(jnp.int32, (400, 128), 1)
        one = jnp.where(lane < 40, v0, jnp.where(lane < 45, v1, 0.0))
        ones = jnp.where((lane >= 90) & (lane < 93), 1.0, 0.0)
        a0[...] = (one + pltpu.roll(one, 45, 1) + ones).astype(BF)
        return g[0:1, 127:128]

    def units(l):
        return [(k, unit_of(l, k), order_of(l, k)) for k in range(taps[l])]

    def slot(l, k):
        return (l % 2) * 3 + k

    def copy0(l, k, u):
        return remote(s0.at[slot(l, k)], r0.at[u], s0_sem.at[u], r0_sem.at[u], peer("core", 1))

    def move0(l, acc):
        for k, u, o in units(l):
            if l + 2 <= 6 and k < taps[l + 2]:
                copy0(l + 2, k, unit_of(l + 2, k)).wait_send()
            keep[u] = acc[pl.ds(pl.multiple_of(k * C + core * 256, 256), 256), :].astype(BF)
            s0[slot(l, k)] = acc[pl.ds(pl.multiple_of(k * C + (1 - core) * 256, 256), 256), :].astype(BF)
            copy0(l, k, u).start()

    def rows64(j):
        return pl.ds(pl.multiple_of(j * 64, 64), 64)

    def rows16(j):
        return pl.ds(pl.multiple_of(j * 16, 16), 16)

    def move1(l):
        for k, u, o in units(l):
            copy0(l, k, u).wait_recv()
            keep[u] = (keep[u].astype(F32) + r0[u].astype(F32)).astype(BF)
            for d in range(1, 4):
                j = lax.rem(at[o[0]] + d, 4)
                remote(keep.at[u, rows64(j)], r1.at[u, d - 1], s1_sem.at[u], r1_sem.at[u], peer(o[0], d)).start()

    def whole(ref, send, recv, o):
        return remote(ref, ref, send, recv, peer(o, 1))

    def move2(l):
        for k, u, o in units(l):
            whole(r1.at[u], s1_sem.at[u], r1_sem.at[u], o[0]).wait_recv()
            v = keep[u, rows64(at[o[0]]), :].astype(F32)
            for d in range(3):
                v = v + r1[u, d].astype(F32)
            h2[u] = v.astype(BF)
            for d in range(1, 4):
                j = lax.rem(at[o[1]] + d, 4)
                remote(h2.at[u, rows16(j)], r2.at[u, d - 1], s2_sem.at[u], r2_sem.at[u], peer(o[1], d)).start()

    def move3(l):
        for k, u, o in units(l):
            whole(r2.at[u], s2_sem.at[u], r2_sem.at[u], o[1]).wait_recv()
            v = h2[u, rows16(at[o[1]]), :].astype(F32)
            for d in range(3):
                v = v + r2[u, d].astype(F32)
            for c in range(4):
                h3[u, c] = v[:, c * 128 : (c + 1) * 128].astype(BF)
            for d in range(1, 4):
                j = lax.rem(at[o[2]] + d, 4)
                remote(h3.at[u, j], r3.at[u, d - 1], s3_sem.at[u], r3_sem.at[u], peer(o[2], d)).start()

    def owners(u, o):
        tile = u * 32 + core * 16 + at[o[0]] * 4 + at[o[1]]
        start = (10 + 16 * tile) * C
        first = lax.div(start, SHARD)
        last = lax.div(start + 8191, SHARD)
        return tile, ((first, True), (last, last != first))

    def final(u, o, i, tile, d):
        s = tile - first_tile(d)
        device = (lax.div(d, 8), lax.rem(d, 8))
        return remote(tl.at[u], own.at[s * 4 + at[o[2]]], t_sem.at[u, i], own_sem.at[s], device)

    def final_here(u, o, tile, d):
        s = tile - first_tile(d)
        return pltpu.make_async_copy(tl.at[u], own.at[s * 4 + at[o[2]]], own_sem.at[s])

    def move4(l):
        for k, u, o in units(l):
            whole(r3.at[u], s3_sem.at[u], r3_sem.at[u], o[2]).wait_recv()
            v = h3[u, at[o[2]]].astype(F32)
            for d in range(3):
                v = v + r3[u, d].astype(F32)
            tl[u] = v
            tile, targets = owners(u, o)
            for i, (d, wanted) in enumerate(targets):
                @pl.when(jnp.logical_and(wanted, d != me))
                def _(u=u, o=o, i=i, tile=tile, d=d):
                    final(u, o, i, tile, d).start()

                @pl.when(jnp.logical_and(wanted, d == me))
                def _(u=u, o=o, tile=tile, d=d):
                    final_here(u, o, tile, d).start()

    moves = (None, move1, move2, move3, move4)

    def emit(l, acc):
        move0(l, acc)
        for stage in range(1, 5):
            if l > 2 and l + stage <= 6:
                moves[stage](l + stage)
        if l == 2:
            for stage in range(1, 5):
                moves[stage](2 + stage)
        if l == 1:
            move2(2)
            move3(3)
            move4(4)

    def between(point):
        if point == 2:
            move1(2)
            move2(3)
            move3(4)
            move4(5)
        elif isinstance(point, tuple):
            i = point[1]
            if i == 0:
                move1(1)
                move3(2)
                move4(3)
            elif i == 1:
                move2(1)
                move4(2)
            elif i == 2:
                move3(1)
            else:
                move4(1)

    fl[...] = jnp.zeros_like(fl)
    encoder_body(
        route, cot, w1, w3_hbm, w2_hbm, bias, gain, shift, emit, between, small,
        a0, w3, w2, wb, gw, [None] + list(xs), list(dgs), [None] + list(xhs), list(rss),
        zs, zt, fs, f4, dz, gn, acc, zt, mm, bandf, wsem,
    )

    def rows_of_core(c):
        return pl.ds(pl.multiple_of(c * 16, 16), 16)

    c0 = remote(small.at[rows_of_core(1 - core)], rs0, q_send.at[0], q_recv.at[0], peer("core", 1))
    c0.start()
    c0.wait()
    v = small[rows_of_core(core), :] + rs0[...]
    for c in range(4):
        hs[c] = v[:, c * 128 : (c + 1) * 128]
    cx = []
    for d in range(1, 4):
        c1 = remote(hs.at[lax.rem(x + d, 4)], rs1.at[d - 1], q_send.at[d], q_recv.at[d], peer("x", d))
        c1.start()
        cx.append(c1)
    v = hs[x]
    for d in range(3):
        cx[d].wait()
        v = v + rs1[d]
    ts[...] = v
    to_last = remote(ts, root.at[me], qr_send.at[0], root_sem.at[0], (15, 7))
    my_last = pltpu.make_async_copy(ts, root.at[me], root_sem.at[0])
    to_zero = remote(ts, root0.at[dp * 4 + x], qr_send.at[1], root_sem.at[1], (0, 0))
    my_zero = pltpu.make_async_copy(ts, root0.at[dp * 4 + x], root_sem.at[1])
    is_last = me == 127
    is_zero = me == 0

    @pl.when(jnp.logical_not(is_last))
    def _():
        to_last.start()

    @pl.when(is_last)
    def _():
        my_last.start()

    @pl.when(jnp.logical_and(core == 0, jnp.logical_not(is_zero)))
    def _():
        to_zero.start()

    @pl.when(is_zero)
    def _():
        my_zero.start()

    low = first_tile(me)
    high = jnp.minimum(lax.div(SHARD * me + SHARD - 1 + 3072, 8192) - 1, 511)

    for s in range(6):
        @pl.when(jnp.logical_and(low + s >= 0, low + s <= high))
        def _(s=s):
            block = own.at[4 * s : 4 * s + 4]
            pltpu.make_async_copy(block, block, own_sem.at[s]).wait()
            for c in range(4):
                fl[pl.ds(64 * s + c, 16, stride=4), :] = own[4 * s + c]

    @pl.when(is_last)
    def _():
        pltpu.make_async_copy(root, root, root_sem.at[0]).wait()
        for c in range(4):
            for h in range(2):
                v = root[2 * c + h]
                for i in range(1, 16):
                    v = v + root[8 * i + 2 * c + h]
                sm4[c, 16 * h : 16 * h + 16, :] = v
            fl[pl.ds(192 + c, 21, stride=4), :] = sm4[c, 10:31, :]

    @pl.when(is_zero)
    def _():
        pltpu.make_async_copy(root0, root0, root_sem.at[1]).wait()
        for c in range(4):
            v = root0[c]
            for i in range(1, 16):
                v = v + root0[4 * i + c]
            sm4[c, 0:16, :] = v
            fl[pl.ds(24 + c, 10, stride=4), :] = sm4[c, 0:10, :]

    offset = SHARD * me - C * (10 + 16 * low)
    row = lax.div(offset, 128)
    turn = lax.rem(offset, 128)
    back = lax.rem(128 - turn, 128)
    upper = pltpu.roll(fl[pl.ds(row, 264), :], back, 1)
    lower = pltpu.roll(fl[pl.ds(row + 1, 264), :], back, 1)
    lane = lax.broadcasted_iota(jnp.int32, (264, 128), 1)
    out[...] = jnp.where(lane < 128 - turn, upper, lower)

    for l in range(1, 7):
        for k, u, o in units(l):
            if l <= 2:
                copy0(l, k, u).wait_send()
            elif k >= taps[l - 2]:
                copy0(l, k, u).wait_send()
            whole(r1.at[u], s1_sem.at[u], r1_sem.at[u], o[0]).wait_send()
            whole(r2.at[u], s2_sem.at[u], r2_sem.at[u], o[1]).wait_send()
            whole(r3.at[u], s3_sem.at[u], r3_sem.at[u], o[2]).wait_send()
            tile, targets = owners(u, o)
            for i, (d, wanted) in enumerate(targets):
                @pl.when(jnp.logical_and(wanted, d != me))
                def _(u=u, o=o, i=i, tile=tile, d=d):
                    final(u, o, i, tile, d).wait_send()

    @pl.when(jnp.logical_not(is_last))
    def _():
        to_last.wait_send()

    @pl.when(jnp.logical_and(core == 0, jnp.logical_not(is_zero)))
    def _():
        to_zero.wait_send()


def comm_scratch():
    dma = pltpu.SemaphoreType.DMA
    return [
        pltpu.VMEM((32, C), F32),
        pltpu.VMEM((8, 144, 128), BF),
        pltpu.VMEM((7, 144, 128), BF),
        pltpu.VMEM((440, 128), F32),
        pltpu.VMEM((6, 256, C), BF),
        pltpu.VMEM((16, 256, C), BF),
        pltpu.VMEM((16, 256, C), BF),
        pltpu.VMEM((16, 3, 64, C), BF),
        pltpu.VMEM((16, 64, C), BF),
        pltpu.VMEM((16, 3, 16, C), BF),
        pltpu.VMEM((16, 4, 16, 128), BF),
        pltpu.VMEM((16, 3, 16, 128), BF),
        pltpu.VMEM((16, 16, 128), F32),
        pltpu.VMEM((24, 16, 128), F32),
        pltpu.VMEM((392, 128), F32),
        pltpu.VMEM((16, C), F32),
        pltpu.VMEM((4, 16, 128), F32),
        pltpu.VMEM((3, 16, 128), F32),
        pltpu.VMEM((16, 128), F32),
        pltpu.VMEM((128, 16, 128), F32),
        pltpu.VMEM((64, 16, 128), F32),
        pltpu.VMEM((4, 32, 128), F32),
        dma((7,)), dma((7,)),
        dma((16,)), dma((16,)), dma((16,)), dma((16,)), dma((16,)), dma((16,)), dma((16,)), dma((16,)),
        dma((16, 2)), dma((6,)),
        dma((4,)), dma((4,)), dma((2,)), dma((2,)),
    ]


def encoder_call(packed, bal, cot, w1, w3, w2, bias, gain, shift):
    vm = pl.BlockSpec(memory_space=pltpu.VMEM)
    sm = pl.BlockSpec(memory_space=pltpu.SMEM)
    hb = pl.BlockSpec(memory_space=pl.ANY)
    return pl.pallas_call(
        encoder_kernel,
        out_shape=jax.ShapeDtypeStruct((264, 128), F32),
        in_specs=[vm, sm, vm, vm, hb, hb, vm, vm, vm],
        out_specs=vm,
        scratch_shapes=body_scratch() + comm_scratch(),
        compiler_params=pltpu.CompilerParams(
            vmem_limit_bytes=64 * 1024 * 1024 - 1024 * 64, collective_id=0, has_side_effects=True
        ),
    )(packed, bal, cot, w1, w3, w2, bias, gain, shift)


def pack_waves(x0, counts):
    frames = counts
    for k, st in ((10, 5), (3, 2), (3, 2), (3, 2), (3, 2), (2, 2), (2, 2)):
        frames = jnp.maximum((frames - k) // st + 1, 0)
    r = jnp.pad(x0.reshape(2, 400, 40), ((0, 0), (0, 32), (0, 0)))
    r = r.reshape(2, 3, 144, 40).transpose(0, 2, 1, 3).reshape(2, 144, 120)
    f = jnp.broadcast_to(frames.astype(BF)[:, None, None], (2, 144, 8))
    return jnp.concatenate([r, f], axis=2)


def normalize_wave(waveforms, lengths):
    positions = jnp.arange(waveforms.shape[1], dtype=jnp.int32)
    valid = (positions[None, :] < lengths[:, None]).astype(F32)
    divisor = jnp.maximum(lengths, 1).astype(F32)
    average = jnp.sum(waveforms * valid, axis=1) / divisor
    centred = (waveforms - average[:, None]) * valid
    spread = jnp.sum(centred * centred, axis=1) / divisor
    return (centred * lax.rsqrt(spread + 1e-07)[:, None]).astype(BF)


def on_device(waveforms, valid_counts, balance_list, cotangent, w_first, w_three, w_two, conv_bias, norm_gain, norm_shift):
    packed = pack_waves(normalize_wave(waveforms, valid_counts), valid_counts)
    shard = encoder_call(
        packed, balance_list, cotangent, w_first,
        w_three.reshape(4, 3 * C, C), w_two.reshape(2, 2 * C, C), conv_bias, norm_gain, norm_shift,
    )
    return shard.reshape(-1)[:SHARD]


def solution(mesh):
    both = ("dp", "narrow")
    in_specs = (
        P(both, None), P(both), P(both), P(both, None, None),
        P(), P(), P(), P(), P(), P(),
    )
    return jax.shard_map(on_device, mesh=mesh, in_specs=in_specs, out_specs=P(both), check_vma=False)
```

time: 531 us -> 105 us (0.20); the launches traced: 523 us -> 104 us
  waiting for transfers between devices: 218 us -> 0 us
  local copies, waits for them, and re-layouts: 117 us -> 2.42 us
  Pallas kernels: 0 us -> 96.6 us
  other arithmetic: 97.1 us -> 5.35 us
  matrix products: 48.8 us -> 0 us
  blocking collectives: 23.2 us -> 0 us
  between operations: 18.6 us -> 0.05 us
    unnamed x2 -> x0, waiting for transfers between devices: 218 us -> none
    pallas_call x0 -> x1, Pallas kernels: none -> 96.6 us  [encoder_call(): pl.pallas_call(encoder_kernel, out_shape=jax.ShapeDtypeStruct((264, 128),...]
    dot_general x34 -> x0, matrix products: 48.8 us -> none  [the longest x7 13.5 us: forward_layer(): jnp.einsum('btk,kc->btc', packed[:, :frames], w_head, preferred_element_t...]
    unnamed x268 -> x1, local copies, waits for them, and re-layouts: 48.1 us -> 1.57 us
    reduce_sum x30 -> x0, other arithmetic: 44.8 us -> none  [the longest x7 29.4 us: post_conv(): normed = centred * lax.rsqrt(spread + 1e-05) * gain_row + shift_row]
    convert_element_type x8 -> x2, other arithmetic: 40.1 us -> 0.86 us  [the longest x1 0.74 us: pack_waves(): f = jnp.broadcast_to(frames.astype(BF)[:, None, None], (2, 144, 8))]
    reshape x16 -> x3, local copies, waits for them, and re-layouts: 28.6 us -> 0.71 us  [the longest x1 0.38 us: pack_waves(): r = jnp.pad(x0.reshape(2, 400, 40), ((0, 0), (0, 32), (0, 0)))]
    dot_general x8 -> x0, local copies, waits for them, and re-layouts: 14.5 us -> none  [backward_layer(): jnp.einsum('btk,btc->kc', packed[:, :frames], grad_low, preferred_element...]
  transfers between devices with their start and end apart: 1 -> 0, of which waited for: 1 -> 0; matrix products, arithmetic and copies ran while one was open for 0% -> 0% of each run, Pallas kernels for 0% -> 0%
where the time goes in v1:
time: 105 us; the launch traced here: 104 us
  Pallas kernels  96.6 us (92%)
  other arithmetic  5.35 us (5%)
  local copies, waits for them, and re-layouts  2.42 us (2%)
    pallas_call x1, Pallas kernels, encoder_call(): pl.pallas_call(encoder_kernel, out_shape=jax.ShapeDtypeStruct((264, 128),...  96.6 us

profile of v1, /device:TPU:0, one launch (start us, length us, event | category | flops | bytes accessed | tf_op | source)
XLA Modules:
  0.0 104.4 jit_solution(13781058875949375823)
XLA Ops:
  0.0 1.2 %select_reduce_fusion = f32[2]{0:T(128)S(1)} fusion(f32[2,16000]{1,0:T(2,128)} %param.10, s32[2]{0:T(128)} %param.11), kind=kLoop, calls=%fused_computation.3 | loop fusion | flops 95998 | bytes 128016 | tf_op jit(solution)/shard_map/reduce_sum | solution.py:740
  1.2 0.7 convert_divide_fusion.1
  1.9 1.2 %multiply_reduce_fusion = (f32[2]{0:T(128)S(1)}, f32[2,16000]{1,0:T(2,128)S(1)}) fusion(f32[2,16000]{1,0:T(2,128)} %param.10, f32[2]{0:T(128)S(1)} %convert_divide_fusion.1, s32[2]{0:T(128)} %param.11), kind=kLoop, calls=%fused_computation.1 | loop fusion | flops 159998 | bytes 256024 | tf_op jit(solution)/shard_map/reduce_sum | solution.py:742
  3.1 0.7 add_rsqrt_fusion
  3.8 0.1 multiply_convert_fusion
  3.9 0.4 reshape.22
  4.3 0.2 copy.14
  4.6 0.1 copy.13
  4.7 0.7 maximum_convert_fusion
  5.4 0.1 broadcast_in_dim.2
  5.5 0.7 pad_maximum_fusion.packed
  6.2 96.6 %shard_map.100 = f32[264,128]{1,0:T(8,128)} custom-call(bf16[2,144,128]{2,1,0:T(8,128)(2,1)} %pad_maximum_fusion.packed, s32[2]{0:T(128)} %bal.1, bf16[1,49,512]{2,1,0:T(8,128)(2,1)} %cot.1, bf16[10,512]{1,0:T(8,128)(2,1)} %w1.1, bf16[4,1536,512]{2,1,0:T(8,128)(2,1)} %bitcast.7, bf16[2,1024,512]{2,1,0:T(8,128)(2,1)} %bitcast.8, f32[7,512]{1,0:T(8,128)} %bias.1, ...), custom_call_target="tpu_custom_call" | custom-call | tf_op jit(solution)/shard_map/pallas_call | solution.py:714
  102.8 1.6 %copy.16 = f32[32892]{0:T(1024)} copy(f32[32892]{0:T(1024)} %bitcast.11) | data formatting | bytes 263136
  (2 shorter events, 0.1 us)
